TPU v7x, 128 devices: a whole 4x4x4 slice. The times are simulated.
128 devices in a mesh: frame: 8 (over x, core), cell: 16 (over y, z).
Axes of the slice: x: 4, y: 4, z: 4, core: 2. Of those that a mesh axis runs over, the one named last changes fastest.
Arguments:
- front: float32 [8, 4096, 4096], P('frame', 'cell')
- parent_of: int32 [8], replicated, may hold values from 0 to 7
- block_map: int32 [8, 13], replicated, may hold values from 3 to 31, as said below
- parent_in: bfloat16 [8, 2, 4096, 8192], P('frame', None, 'cell'), may hold values from -0.3125 to 0.3125
Outputs:
- lower_panel: float32 [8, 4096, 768], P('frame', 'cell')
- parent_out: bfloat16 [8, 2, 4096, 8192], P('frame', None, 'cell')
Inputs may be any that keep to these rules, and one draw needn't show every extreme that they name: block_map[c, k] is 3 + k or 3 + k + 16.
All inputs are finite; a program needn't handle non-finite values.
Results may differ from a plain program's by a relative error of at most 0.004.
Values may be sent and summed in bfloat16 or wider, within the bound.
A program may use at most 192 MiB of HBM per device.

v0:
```python
import jax
import jax.numpy as jnp
from jax import lax
from jax.sharding import PartitionSpec as P

PB = 3


def per_device(front, parent_of, block_map, parent_in):
    block_row = front[0]
    rows_here = block_row.shape[0]
    order = block_row.shape[1]
    blocks = order // rows_here
    width = PB * rows_here
    cell_index = lax.axis_index("cell")
    frame_index = lax.axis_index("frame")
    highest = lax.Precision.HIGHEST
    panel = lax.all_gather(block_row[:, :width], "cell", axis=0, tiled=True)
    l11 = jnp.linalg.cholesky(panel[:width])
    l21 = lax.linalg.triangular_solve(
        l11, panel[width:], left_side=False, lower=True, transpose_a=True
    )
    lower_all = jnp.concatenate([l11, l21], 0)
    my_lower = lax.dynamic_slice_in_dim(lower_all, cell_index * rows_here, rows_here, 0)
    product = jnp.dot(my_lower, l21.T, precision=highest)
    update = (block_row[:, width:] - product).astype(jnp.bfloat16)
    update_blocks = update.shape[1] // rows_here
    which_k = jnp.maximum(cell_index - PB, 0)
    whole_parent = parent_in[0].reshape(2, rows_here, 2, blocks, rows_here)
    region_start = whole_parent[:, :, :, PB:, :].astype(jnp.float32)
    pieces = lax.all_gather(update[None], "frame", axis=0, tiled=True)

    def one_child(step, acc):
        parent = lax.dynamic_index_in_dim(parent_of, step, 0, keepdims=False)
        positions = lax.dynamic_index_in_dim(block_map, step, 0, keepdims=False)
        target = lax.dynamic_index_in_dim(positions, which_k, 0, keepdims=False)
        live = (parent == frame_index) & (cell_index >= PB)
        half = target // blocks

        def add_piece(inner):
            piece = lax.dynamic_index_in_dim(pieces, step, 0, keepdims=False)
            piece = piece.reshape(rows_here, update_blocks, rows_here).astype(jnp.float32)
            upper = (positions >= blocks)[None, :, None]
            zeros = jnp.zeros_like(piece)
            delta = jnp.stack([jnp.where(upper, zeros, piece), jnp.where(upper, piece, zeros)], 1)
            current = lax.dynamic_index_in_dim(inner, half, 0, keepdims=False)
            return lax.dynamic_update_index_in_dim(inner, current + delta, half, 0)

        def keep_same(inner):
            return inner

        return lax.cond(live, add_piece, keep_same, acc)

    total = lax.fori_loop(0, pieces.shape[0], one_child, region_start)
    merged = jnp.concatenate([whole_parent[:, :, :, :PB, :], total.astype(jnp.bfloat16)], 3)
    merged = merged.reshape(2, rows_here, 2 * blocks * rows_here)
    return (my_lower[None], merged[None])


def solution(mesh):
    placed = (P("frame", "cell", None), P(), P(), P("frame", None, "cell", None))
    return jax.shard_map(
        per_device,
        mesh=mesh,
        in_specs=placed,
        out_specs=(P("frame", "cell", None), P("frame", None, "cell", None)),
        check_vma=False,
    )
```

profile of v0, /device:TPU:15, one launch (start us, length us, event | category | flops | bytes accessed | tf_op | source)
XLA Modules:
  0.0 594.5 jit_solution(12432647070224209038)
XLA Ops:
  7.2 5.6 copy.11
  15.0 101.0 %all-gather.4.cloned.1.call-done = f32[4096,768]{0,1:T(8,128)} async-done(((f32[256,768]{0,1:T(8,128)}), f32[4096,768]{0,1:T(8,128)}) %all-gather.4.cloned.1.call-update) | async-done | bytes 12582928 | tf_op jit(solution)/shard_map/all_gather | solution.py:18
  123.7 11.7 %cholesky.165 = f32[128,128]{1,0:T(8,128)S(1)} custom-call(f32[128,128]{1,0:T(8,128)S(1)} %cholesky.424), custom_call_target="Cholesky" | custom-call | tf_op jit(solution)/shard_map/jit(cholesky)/cholesky | solution.py:19
  135.4 9.8 %custom-call.46 = f32[1,128,128]{1,2,0:T(8,128)S(1)} custom-call(f32[1,128,128]{2,1,0:T(8,128)S(1)} %get-tuple-element.497), custom_call_target="InvertDiagBlocksLowerTriangular" | custom-call | tf_op jit(solution)/shard_map/jit(cholesky)/cholesky | solution.py:19
  148.2 11.7 %cholesky.188 = f32[128,128]{1,0:T(8,128)S(1)} custom-call(f32[128,128]{1,0:T(8,128)S(1)} %cholesky.428), custom_call_target="Cholesky" | custom-call | tf_op jit(solution)/shard_map/jit(cholesky)/cholesky | solution.py:19
  160.0 10.1 %custom-call.47 = f32[1,128,128]{1,2,0:T(8,128)S(1)} custom-call(f32[1,128,128]{2,1,0:T(8,128)S(1)} %get-tuple-element.494), custom_call_target="InvertDiagBlocksLowerTriangular" | custom-call | tf_op jit(solution)/shard_map/jit(cholesky)/cholesky | solution.py:19
  172.0 11.7 %cholesky.354 = f32[128,128]{1,0:T(8,128)S(1)} custom-call(f32[128,128]{1,0:T(8,128)S(1)} %cholesky.433), custom_call_target="Cholesky" | custom-call | tf_op jit(solution)/shard_map/jit(cholesky)/cholesky | solution.py:19
  184.4 9.8 %custom-call.48 = f32[1,128,128]{1,2,0:T(8,128)S(1)} custom-call(f32[1,128,128]{2,1,0:T(8,128)S(1)} %get-tuple-element.491), custom_call_target="InvertDiagBlocksLowerTriangular" | custom-call | tf_op jit(solution)/shard_map/jit(cholesky)/cholesky | solution.py:19
  196.1 11.9 %cholesky.373 = f32[128,128]{1,0:T(8,128)S(1)} custom-call(f32[128,128]{1,0:T(8,128)S(1)} %cholesky.438), custom_call_target="Cholesky" | custom-call | tf_op jit(solution)/shard_map/jit(cholesky)/cholesky | solution.py:19
  208.7 9.8 %custom-call.49 = f32[1,128,128]{1,2,0:T(8,128)S(1)} custom-call(f32[1,128,128]{2,1,0:T(8,128)S(1)} %get-tuple-element.488), custom_call_target="InvertDiagBlocksLowerTriangular" | custom-call | tf_op jit(solution)/shard_map/jit(cholesky)/cholesky | solution.py:19
  220.3 11.7 %cholesky.392 = f32[128,128]{1,0:T(8,128)S(1)} custom-call(f32[128,128]{1,0:T(8,128)S(1)} %cholesky.443), custom_call_target="Cholesky" | custom-call | tf_op jit(solution)/shard_map/jit(cholesky)/cholesky | solution.py:19
  232.7 9.8 %custom-call.50 = f32[1,128,128]{1,2,0:T(8,128)S(1)} custom-call(f32[1,128,128]{2,1,0:T(8,128)S(1)} %get-tuple-element.485), custom_call_target="InvertDiagBlocksLowerTriangular" | custom-call | tf_op jit(solution)/shard_map/jit(cholesky)/cholesky | solution.py:19
  244.0 12.1 %cholesky.410 = f32[128,128]{1,0:T(8,128)S(1)} custom-call(f32[128,128]{1,0:T(8,128)S(1)} %convolution_subtract_fusion.8), custom_call_target="Cholesky" | custom-call | tf_op jit(solution)/shard_map/jit(cholesky)/cholesky | solution.py:19
  263.5 17.4 %while.21 = (s32[]{:T(128)}, f32[768,768]{1,0:T(8,128)}, s32[6,2]{0,1:T(2,128)S(1)}, f32[6,128,128]{2,1,0:T(8,128)S(1)}, s32[]{:T(128)}) while((s32[]{:T(128)}, f32[768,768]{1,0:T(8,128)}, s32[6,2]{0,1:T(2,128)S(1)}, f32[6,128,128]{2,1,0:T(8,128)S(1)}, s32[]{:T(128)}) %tuple.115), condition=%wide.while_cond, body=%wide.while_body.sunk | while | flops 2 | bytes 131181 | solution.py:20
  281.0 59.0 %custom-call.51 = f32[6,128,128]{1,2,0:T(8,128)S(1)} custom-call(f32[6,128,128]{2,1,0:T(8,128)S(1)} %get-tuple-element.425), custom_call_target="InvertDiagBlocksLowerTriangular" | custom-call | tf_op jit(solution)/shard_map/triangular_solve | solution.py:20
  369.2 7.1 %fusion.19 = f32[3328,128]{0,1:T(8,128)} fusion(f32[3328,128]{0,1:T(8,128)} %get-tuple-element.503, f32[3328,128]{0,1:T(8,128)} %copy-done.2, f32[3328,128]{0,1:T(8,128)S(1)} %get-tuple-element.501, f32[3328,128]{0,1:T(8,128)S(1)} %bitcast.107, f32[4096,768]{0,1:T(8,128)S(1)} %bitcast.111, f32[768,768]{1,0:T(8,128)} %get-tuple-element.639), kind=kOutput, calls=%fused_computation.35 | convolution fusion | flops 2622783488 | bytes 10485760 | tf_op jit(solution)/shard_map/triangular_solve | solution.py:20
  380.6 8.5 %convolution_subtract_fusion.1 = f32[3328,128]{0,1:T(8,128)S(1)} fusion(f32[3328,640]{0,1:T(8,128)} %get-tuple-element.472, f32[4096,768]{0,1:T(8,128)S(1)} %bitcast.111, f32[768,768]{1,0:T(8,128)} %get-tuple-element.639), kind=kOutput, calls=%fused_computation.31 | convolution fusion | flops 3271983104 | bytes 12255232 | tf_op jit(solution)/shard_map/triangular_solve | solution.py:20
  393.8 18.2 %fusion.9 = bf16[256,3328]{0,1:T(8,128)(2,1)} fusion(f32[256,768]{0,1:T(8,128)S(1)} %fusion.29, f32[3328,768]{0,1:T(8,128)S(1)} %convolution_dynamic-update-slice_fusion, f32[256,4096]{0,1:T(8,128)S(1)} %bitcast.109), kind=kOutput, calls=%fused_computation.24 | convolution fusion | flops 7853441024 | bytes 16121856 | tf_op jit(solution)/shard_map/dot_general | solution.py:25
  412.0 12.0 %copy.15 = bf16[1,2,256,8192]{2,3,1,0:T(8,128)(2,1)} copy(bf16[1,2,256,8192]{3,2,1,0:T(8,128)(2,1)} %param.11) | data formatting | bytes 16777216 | tf_op args[3]
  425.7 9.8 %slice_convert_fusion = f32[2,256,2,13,256]{1,4,3,2,0:T(8,128)} fusion(bf16[2,256,2,16,256]{1,4,3,2,0:T(8,128)(2,1)} %bitcast.103), kind=kLoop, calls=%fused_computation.13 | loop fusion | flops 3407872 | bytes 20447232 | tf_op jit(solution)/shard_map/convert_element_type | solution.py:30
  436.7 52.1 %all-gather.6.cloned.1.call-done = bf16[2048,3328]{0,1:T(8,128)(2,1)} async-done(((bf16[256,3328]{0,1:T(8,128)(2,1)}), bf16[2048,3328]{0,1:T(8,128)(2,1)}) %all-gather.6.cloned.1.call-update) | async-done | bytes 13631504 | tf_op jit(solution)/shard_map/all_gather | solution.py:31
  488.8 12.5 %copy.23 = bf16[416,8,8,256]{3,2,0,1:T(8,128)(2,1)} copy(bf16[416,8,8,256]{3,2,1,0:T(8,128)(2,1)} %bitcast.112) | data formatting | bytes 27262976 | tf_op jit(solution)/shard_map/all_gather | solution.py:31
  501.3 58.4 %while.20 = (s32[]{:T(128)}, f32[2,256,2,13,256]{1,4,3,2,0:T(8,128)}, s32[8]{0:T(128)S(1)}, s32[]{:T(128)}, pred[]{:T(512)}, /*index=5*/s32[8,13]{1,0:T(8,128)},...) while((s32[]{:T(128)}, f32[2,256,2,13,256]{1,4,3,2,0:T(8,128)}, ...), condition=%wide.region_15.16_spmd, body=%wide.region_12.15_spmd.sunk | while | flops 5963816 | bytes 32375320 | solution.py:54
  504.1 12.4 %conditional.2 = (f32[2,256,2,13,256]{1,4,3,2,0:T(8,128)}) conditional(s32[]{:T(128)} %convert_element_type.50, f32[2,256,2,13,256]{1,4,3,2,0:T(8,128)} %get-tuple-element.611, (s32[]{:T(128)}, s32[]{:T(128)}, f32[2,256,2,13,256]{1,4,3,2,0:T(8,128)}, s32[8,13]{1,0:T(8,128)}, s32[]{:T(128)}, /*index=5*/bf16[8,256,3328]{1,2,0:T(8,128)(2,1)}, ...), branch_computations={%region_13.13_spmd, %region_14.14_spmd} | conditional | flops 5963810 | bytes 32375100 | solution.py:52
  509.9 6.6 %fusion = f32[2,256,2,13,256]{1,4,3,2,0:T(8,128)} fusion(f32[2,256,2,13,256]{1,4,3,2,0:T(8,128)} %get-tuple-element.397, s32[]{:T(128)S(6)} %select_n.87, f32[1,256,1,13,256]{1,4,3,2,0:T(8,128)S(1)} %get-tuple-element.469, f32[1,256,1,13,256]{1,4,3,2,0:T(8,128)S(1)} %get-tuple-element.468), kind=kLoop, calls=%fused_computation.1 | loop fusion | flops 3407872 | bytes 20447236 | tf_op jit(solution)/shard_map/while/body/eval_jaxpr/cond/branch_1_fun/jit(dynamic_update_index_in_dim)/dynamic_update_slice | solution.py:47
  527.0 12.5 %conditional.2 = (f32[2,256,2,13,256]{1,4,3,2,0:T(8,128)}) conditional(s32[]{:T(128)} %convert_element_type.50, f32[2,256,2,13,256]{1,4,3,2,0:T(8,128)} %get-tuple-element.611, (s32[]{:T(128)}, s32[]{:T(128)}, f32[2,256,2,13,256]{1,4,3,2,0:T(8,128)}, s32[8,13]{1,0:T(8,128)}, s32[]{:T(128)}, /*index=5*/bf16[8,256,3328]{1,2,0:T(8,128)(2,1)}, ...), branch_computations={%region_13.13_spmd, %region_14.14_spmd} | conditional | flops 5963810 | bytes 32375100 | solution.py:52
  532.8 6.6 %fusion = f32[2,256,2,13,256]{1,4,3,2,0:T(8,128)} fusion(f32[2,256,2,13,256]{1,4,3,2,0:T(8,128)} %get-tuple-element.397, s32[]{:T(128)S(6)} %select_n.87, f32[1,256,1,13,256]{1,4,3,2,0:T(8,128)S(1)} %get-tuple-element.469, f32[1,256,1,13,256]{1,4,3,2,0:T(8,128)S(1)} %get-tuple-element.468), kind=kLoop, calls=%fused_computation.1 | loop fusion | flops 3407872 | bytes 20447236 | tf_op jit(solution)/shard_map/while/body/eval_jaxpr/cond/branch_1_fun/jit(dynamic_update_index_in_dim)/dynamic_update_slice | solution.py:47
  542.0 12.4 %conditional.2 = (f32[2,256,2,13,256]{1,4,3,2,0:T(8,128)}) conditional(s32[]{:T(128)} %convert_element_type.50, f32[2,256,2,13,256]{1,4,3,2,0:T(8,128)} %get-tuple-element.611, (s32[]{:T(128)}, s32[]{:T(128)}, f32[2,256,2,13,256]{1,4,3,2,0:T(8,128)}, s32[8,13]{1,0:T(8,128)}, s32[]{:T(128)}, /*index=5*/bf16[8,256,3328]{1,2,0:T(8,128)(2,1)}, ...), branch_computations={%region_13.13_spmd, %region_14.14_spmd} | conditional | flops 5963810 | bytes 32375100 | solution.py:52
  547.8 6.6 %fusion = f32[2,256,2,13,256]{1,4,3,2,0:T(8,128)} fusion(f32[2,256,2,13,256]{1,4,3,2,0:T(8,128)} %get-tuple-element.397, s32[]{:T(128)S(6)} %select_n.87, f32[1,256,1,13,256]{1,4,3,2,0:T(8,128)S(1)} %get-tuple-element.469, f32[1,256,1,13,256]{1,4,3,2,0:T(8,128)S(1)} %get-tuple-element.468), kind=kLoop, calls=%fused_computation.1 | loop fusion | flops 3407872 | bytes 20447236 | tf_op jit(solution)/shard_map/while/body/eval_jaxpr/cond/branch_1_fun/jit(dynamic_update_index_in_dim)/dynamic_update_slice | solution.py:47
  559.6 8.7 %convert_element_type.45 = bf16[2,256,2,13,256]{1,4,3,2,0:T(8,128)(2,1)} convert(f32[2,256,2,13,256]{1,4,3,2,0:T(8,128)} %get-tuple-element.415) | non-fusion elementwise | flops 3407872 | bytes 20447232 | tf_op jit(solution)/shard_map/convert_element_type | solution.py:55
  568.4 6.9 %pad_maximum_fusion = bf16[2,256,2,16,256]{1,4,3,2,0:T(8,128)(2,1)} fusion(bf16[2,256,2,13,256]{1,4,3,2,0:T(8,128)(2,1)} %convert_element_type.45, bf16[2,256,2,3,256]{1,4,3,2,0:T(8,128)(2,1)S(1)} %slice.203), kind=kLoop, calls=%fused_computation.12 | loop fusion | flops 4194304 | bytes 16777216 | tf_op jit(solution)/shard_map/concatenate | solution.py:55
  575.2 12.0 %copy.20 = bf16[1,2,256,8192]{3,2,1,0:T(8,128)(2,1)} copy(bf16[1,2,256,8192]{2,3,1,0:T(8,128)(2,1)} %bitcast.104) | data formatting | bytes 16777216 | tf_op jit(solution)/shard_map/broadcast_in_dim;reshape | solution.py:57
  (120 shorter events, 108.9 us)
Async XLA Ops:
  7.2 108.8 %all-gather.4.cloned.1.call-start = ((), (), s32[]{:S(2)}) async-start(), calls=%async_computation | async-start | bytes 13369344 | tf_op jit(solution)/shard_map/all_gather | solution.py:18
  14.9 473.9 %all-gather.6.cloned.1.call-start = ((), (), s32[]{:S(2)}) async-start(), calls=%async_computation.1 | async-start | bytes 15335424 | tf_op jit(solution)/shard_map/all_gather | solution.py:31
  115.9 1.7 slice-start.3
  122.3 1.4 copy-start.3
  339.9 8.6 %copy-start.4 = (f32[6,128,128]{1,2,0:T(8,128)}, f32[6,128,128]{1,2,0:T(8,128)S(1)}, u32[]{:S(2)}) copy-start(f32[6,128,128]{1,2,0:T(8,128)S(1)} %custom-call.51) | copy-start | bytes 1179652
  345.2 14.6 %slice-start = ((s8[12582912]{0:T(1024)(128)(4,1)}), s8[4194304]{0:T(1024)(128)(4,1)S(1)}, s32[]{:S(2)}) async-start(s8[12582912]{0:T(1024)(128)(4,1)} %bitcast.110), calls=%async_computation.2 | async-start | bytes 8388608
  348.5 11.3 %slice-start.1 = ((s8[12582912]{0:T(1024)(128)(4,1)}), s8[4194304]{0:T(1024)(128)(4,1)S(1)}, s32[]{:S(2)}) async-start(s8[12582912]{0:T(1024)(128)(4,1)} %bitcast.110), calls=%async_computation.3 | async-start | bytes 8388608
  350.3 9.6 %slice-start.2 = ((s8[12582912]{0:T(1024)(128)(4,1)}), s8[4194304]{0:T(1024)(128)(4,1)S(1)}, s32[]{:S(2)}) async-start(s8[12582912]{0:T(1024)(128)(4,1)} %bitcast.110), calls=%async_computation.4 | async-start | bytes 8388608
  356.6 3.2 copy-start.1
  359.9 5.0 copy-start.2
  391.6 2.2 copy-start
  488.8 12.5 %copy-start.5 = (s32[8]{0:T(128)S(1)}, s32[8]{0:T(128)}, u32[]{:S(2)}) copy-start(s32[8]{0:T(128)} %param.9) | copy-start | bytes 100
Sparse Core Ops, SparseCore 0:
  15.0 100.8 all-gather.3
  412.1 76.6 all-gather.5
where the time goes:
time: 606 us; the launch traced here: 594 us
  other arithmetic  238 us (39%)
  waiting for transfers between devices  153 us (25%)
  local copies, waits for them, and re-layouts  97.1 us (16%)
  matrix products  74 us (12%)
  between operations  18.5 us (3%)
  loops' own time  14 us (2%)
    another operation x22, other arithmetic, per_device(): l11 = jnp.linalg.cholesky(panel[:width])  124 us
    all_gather x1, waiting for transfers between devices, per_device(): panel = lax.all_gather(block_row[:, :width], 'cell', axis=0, tiled=True)  101 us
    another operation x3, other arithmetic, per_device(): lax.linalg.triangular_solve(l11, panel[width:], left_side=False, lower=Tr...  61.4 us
    all_gather x1, waiting for transfers between devices, per_device(): pieces = lax.all_gather(update[None], 'frame', axis=0, tiled=True)  52.1 us
    another operation x11, matrix products, per_device(): lax.linalg.triangular_solve(l11, panel[width:], left_side=False, lower=Tr...  46.1 us
    unnamed x20, local copies, waits for them, and re-layouts  24.3 us
    dynamic_update_slice x3, other arithmetic, add_piece(): return lax.dynamic_update_index_in_dim(inner, current + delta, half, 0)  19.8 us
    dot_general x1, matrix products, per_device(): product = jnp.dot(my_lower, l21.T, precision=highest)  18.2 us
  transfers between devices with their start and end apart: 2, of which 2 were waited for; matrix products, arithmetic and copies ran while one was open for 4% of the time, Pallas kernels for 0%

commit v1 on v0

--- a/solution.py
+++ b/solution.py
@@ -28,7 +28,14 @@
     which_k = jnp.maximum(cell_index - PB, 0)
     whole_parent = parent_in[0].reshape(2, rows_here, 2, blocks, rows_here)
     region_start = whole_parent[:, :, :, PB:, :].astype(jnp.float32)
-    pieces = lax.all_gather(update[None], "frame", axis=0, tiled=True)
+    ring = [update[None]]
+    for hop in range(7):
+        ring.append(lax.ppermute(ring[-1], "frame", [(dev, (dev + 1) % 8) for dev in range(8)]))
+    pieces = jnp.roll(
+        jnp.concatenate(ring[::-1], axis=0),
+        (lax.axis_index("frame") + 1) * ring[0].shape[0],
+        axis=0,
+    )
 
     def one_child(step, acc):
         parent = lax.dynamic_index_in_dim(parent_of, step, 0, keepdims=False)

time: 606 us -> 702 us (1.16)
  waiting for transfers between devices: 153 us -> 214 us
  starting transfers between devices: 0.08 us -> 24 us
  local copies, waits for them, and re-layouts: 97.1 us -> 110 us
    ppermute x0 -> x7, waiting for transfers between devices: none -> 113 us  [per_device(): lax.ppermute(ring[-1], 'frame', [(dev, (dev + 1) % 8) for dev in range(8)])]
    all_gather x1 -> x0, waiting for transfers between devices: 52.1 us -> none  [per_device(): pieces = lax.all_gather(update[None], 'frame', axis=0, tiled=True)]
    ppermute x0 -> x7, starting transfers between devices: none -> 24 us  [per_device(): lax.ppermute(ring[-1], 'frame', [(dev, (dev + 1) % 8) for dev in range(8)])]
    unnamed x20 -> x61, local copies, waits for them, and re-layouts: 24.3 us -> 43.5 us
    all_gather x1 -> x0, local copies, waits for them, and re-layouts: 12.5 us -> none  [per_device(): pieces = lax.all_gather(update[None], 'frame', axis=0, tiled=True)]
  transfers between devices with their start and end apart: 2 -> 8, of which waited for: 2 -> 7; matrix products, arithmetic and copies ran while one was open for 4% -> 4% of each run, Pallas kernels for 0% -> 0%
where the time goes in v1:
time: 702 us; the launch traced here: 690 us
  other arithmetic  238 us (34%)
  waiting for transfers between devices  214 us (30%)
  local copies, waits for them, and re-layouts  110 us (16%)
  matrix products  73.6 us (10%)
  starting transfers between devices  24 us (3%)
  between operations  18.7 us (3%)
  loops' own time  12.3 us (2%)
    another operation x22, other arithmetic, per_device(): l11 = jnp.linalg.cholesky(panel[:width])  124 us
    ppermute x7, waiting for transfers between devices, per_device(): lax.ppermute(ring[-1], 'frame', [(dev, (dev + 1) % 8) for dev in range(8)])  113 us
    all_gather x1, waiting for transfers between devices, per_device(): panel = lax.all_gather(block_row[:, :width], 'cell', axis=0, tiled=True)  101 us
    another operation x3, other arithmetic, per_device(): lax.linalg.triangular_solve(l11, panel[width:], left_side=False, lower=Tr...  61.4 us
    another operation x11, matrix products, per_device(): lax.linalg.triangular_solve(l11, panel[width:], left_side=False, lower=Tr...  46.3 us
    unnamed x61, local copies, waits for them, and re-layouts  43.5 us
    ppermute x7, starting transfers between devices, per_device(): lax.ppermute(ring[-1], 'frame', [(dev, (dev + 1) % 8) for dev in range(8)])  24 us
    dynamic_update_slice x3, other arithmetic, add_piece(): return lax.dynamic_update_index_in_dim(inner, current + delta, half, 0)  19.8 us
  transfers between devices with their start and end apart: 8, of which 7 were waited for; matrix products, arithmetic and copies ran while one was open for 4% of the time, Pallas kernels for 0%

profile of v1, /device:TPU:15, one launch (start us, length us, event | category | flops | bytes accessed | tf_op | source)
XLA Modules:
  0.0 690.3 jit_solution(11636617548586124716)
XLA Ops:
  14.9 101.0 %all-gather.2.cloned.1.call-done = f32[4096,768]{0,1:T(8,128)} async-done(((f32[256,768]{0,1:T(8,128)}), f32[4096,768]{0,1:T(8,128)}) %all-gather.2.cloned.1.call-update) | async-done | bytes 12582928 | tf_op jit(solution)/shard_map/all_gather | solution.py:18
  123.6 11.7 %cholesky.165 = f32[128,128]{1,0:T(8,128)S(1)} custom-call(f32[128,128]{1,0:T(8,128)S(1)} %cholesky.424), custom_call_target="Cholesky" | custom-call | tf_op jit(solution)/shard_map/jit(cholesky)/cholesky | solution.py:19
  135.4 9.8 %custom-call.46 = f32[1,128,128]{1,2,0:T(8,128)S(1)} custom-call(f32[1,128,128]{2,1,0:T(8,128)S(1)} %get-tuple-element.489), custom_call_target="InvertDiagBlocksLowerTriangular" | custom-call | tf_op jit(solution)/shard_map/jit(cholesky)/cholesky | solution.py:19
  148.2 11.7 %cholesky.188 = f32[128,128]{1,0:T(8,128)S(1)} custom-call(f32[128,128]{1,0:T(8,128)S(1)} %cholesky.428), custom_call_target="Cholesky" | custom-call | tf_op jit(solution)/shard_map/jit(cholesky)/cholesky | solution.py:19
  159.9 9.9 %custom-call.47 = f32[1,128,128]{1,2,0:T(8,128)S(1)} custom-call(f32[1,128,128]{2,1,0:T(8,128)S(1)} %get-tuple-element.486), custom_call_target="InvertDiagBlocksLowerTriangular" | custom-call | tf_op jit(solution)/shard_map/jit(cholesky)/cholesky | solution.py:19
  171.8 11.7 %cholesky.354 = f32[128,128]{1,0:T(8,128)S(1)} custom-call(f32[128,128]{1,0:T(8,128)S(1)} %cholesky.433), custom_call_target="Cholesky" | custom-call | tf_op jit(solution)/shard_map/jit(cholesky)/cholesky | solution.py:19
  184.2 9.8 %custom-call.48 = f32[1,128,128]{1,2,0:T(8,128)S(1)} custom-call(f32[1,128,128]{2,1,0:T(8,128)S(1)} %get-tuple-element.483), custom_call_target="InvertDiagBlocksLowerTriangular" | custom-call | tf_op jit(solution)/shard_map/jit(cholesky)/cholesky | solution.py:19
  196.0 12.1 %cholesky.373 = f32[128,128]{1,0:T(8,128)S(1)} custom-call(f32[128,128]{1,0:T(8,128)S(1)} %cholesky.438), custom_call_target="Cholesky" | custom-call | tf_op jit(solution)/shard_map/jit(cholesky)/cholesky | solution.py:19
  208.7 9.8 %custom-call.49 = f32[1,128,128]{1,2,0:T(8,128)S(1)} custom-call(f32[1,128,128]{2,1,0:T(8,128)S(1)} %get-tuple-element.480), custom_call_target="InvertDiagBlocksLowerTriangular" | custom-call | tf_op jit(solution)/shard_map/jit(cholesky)/cholesky | solution.py:19
  220.3 11.7 %cholesky.392 = f32[128,128]{1,0:T(8,128)S(1)} custom-call(f32[128,128]{1,0:T(8,128)S(1)} %cholesky.443), custom_call_target="Cholesky" | custom-call | tf_op jit(solution)/shard_map/jit(cholesky)/cholesky | solution.py:19
  232.7 9.8 %custom-call.50 = f32[1,128,128]{1,2,0:T(8,128)S(1)} custom-call(f32[1,128,128]{2,1,0:T(8,128)S(1)} %get-tuple-element.477), custom_call_target="InvertDiagBlocksLowerTriangular" | custom-call | tf_op jit(solution)/shard_map/jit(cholesky)/cholesky | solution.py:19
  244.1 11.9 %cholesky.410 = f32[128,128]{1,0:T(8,128)S(1)} custom-call(f32[128,128]{1,0:T(8,128)S(1)} %convolution_subtract_fusion.8), custom_call_target="Cholesky" | custom-call | tf_op jit(solution)/shard_map/jit(cholesky)/cholesky | solution.py:19
  263.5 18.1 %while.21 = (s32[]{:T(128)}, f32[768,768]{1,0:T(8,128)}, s32[6,2]{0,1:T(2,128)S(1)}, f32[6,128,128]{2,1,0:T(8,128)S(1)}, s32[]{:T(128)}) while((s32[]{:T(128)}, f32[768,768]{1,0:T(8,128)}, s32[6,2]{0,1:T(2,128)S(1)}, f32[6,128,128]{2,1,0:T(8,128)S(1)}, s32[]{:T(128)}) %tuple.114), condition=%wide.while_cond, body=%wide.while_body.sunk | while | flops 2 | bytes 131181 | solution.py:20
  281.7 59.0 %custom-call.51 = f32[6,128,128]{1,2,0:T(8,128)S(1)} custom-call(f32[6,128,128]{2,1,0:T(8,128)S(1)} %get-tuple-element.425), custom_call_target="InvertDiagBlocksLowerTriangular" | custom-call | tf_op jit(solution)/shard_map/triangular_solve | solution.py:20
  370.2 7.2 %fusion.20 = f32[3328,128]{0,1:T(8,128)} fusion(f32[3328,128]{0,1:T(8,128)} %get-tuple-element.495, f32[3328,128]{0,1:T(8,128)} %copy-done.14, f32[3328,128]{0,1:T(8,128)S(1)} %get-tuple-element.493, f32[3328,128]{0,1:T(8,128)S(1)} %bitcast.104, f32[4096,768]{0,1:T(8,128)S(1)} %bitcast.108, f32[768,768]{1,0:T(8,128)} %get-tuple-element.638), kind=kOutput, calls=%fused_computation.35 | convolution fusion | flops 2622783488 | bytes 10485760 | tf_op jit(solution)/shard_map/triangular_solve | solution.py:20
  381.6 8.4 %convolution_subtract_fusion.1 = f32[3328,128]{0,1:T(8,128)S(1)} fusion(f32[3328,640]{0,1:T(8,128)} %get-tuple-element.464, f32[4096,768]{0,1:T(8,128)S(1)} %bitcast.108, f32[768,768]{1,0:T(8,128)} %get-tuple-element.638), kind=kOutput, calls=%fused_computation.30 | convolution fusion | flops 3271983104 | bytes 12255232 | tf_op jit(solution)/shard_map/triangular_solve | solution.py:20
  394.7 17.5 %fusion.16 = bf16[1,256,3328]{1,2,0:T(8,128)(2,1)S(1)} fusion(f32[256,768]{0,1:T(8,128)S(1)} %fusion.30, f32[3328,768]{0,1:T(8,128)S(1)} %convolution_dynamic-update-slice_fusion, f32[256,4096]{0,1:T(8,128)S(1)} %bitcast.106), kind=kOutput, calls=%fused_computation.33 | convolution fusion | flops 7853441024 | bytes 16121856 | tf_op jit(solution)/shard_map/dot_general | solution.py:25
  413.9 18.8 %collective-permute-done = bf16[1,256,3328]{1,2,0:T(8,128)(2,1)S(1)} collective-permute-done((bf16[1,256,3328]{1,2,0:T(8,128)(2,1)S(1)}, bf16[1,256,3328]{1,2,0:T(8,128)(2,1)S(1)}, u32[]{:S(2)}, u32[]{:S(2)}) %collective-permute-start) | collective-permute-done | bytes 1703968 | tf_op jit(solution)/shard_map/ppermute | solution.py:33
  437.6 18.8 %collective-permute-done.1 = bf16[1,256,3328]{1,2,0:T(8,128)(2,1)S(1)} collective-permute-done((bf16[1,256,3328]{1,2,0:T(8,128)(2,1)S(1)}, bf16[1,256,3328]{1,2,0:T(8,128)(2,1)S(1)}, u32[]{:S(2)}, u32[]{:S(2)}) %collective-permute-start.1) | collective-permute-done | bytes 1703968 | tf_op jit(solution)/shard_map/ppermute | solution.py:33
  461.3 18.8 %collective-permute-done.2 = bf16[1,256,3328]{1,2,0:T(8,128)(2,1)S(1)} collective-permute-done((bf16[1,256,3328]{1,2,0:T(8,128)(2,1)S(1)}, bf16[1,256,3328]{1,2,0:T(8,128)(2,1)S(1)}, u32[]{:S(2)}, u32[]{:S(2)}) %collective-permute-start.2) | collective-permute-done | bytes 1703968 | tf_op jit(solution)/shard_map/ppermute | solution.py:33
  484.9 18.8 %collective-permute-done.3 = bf16[1,256,3328]{1,2,0:T(8,128)(2,1)S(1)} collective-permute-done((bf16[1,256,3328]{1,2,0:T(8,128)(2,1)S(1)}, bf16[1,256,3328]{1,2,0:T(8,128)(2,1)S(1)}, u32[]{:S(2)}, u32[]{:S(2)}) %collective-permute-start.3) | collective-permute-done | bytes 1703968 | tf_op jit(solution)/shard_map/ppermute | solution.py:33
  508.6 18.8 %collective-permute-done.4 = bf16[1,256,3328]{1,2,0:T(8,128)(2,1)S(1)} collective-permute-done((bf16[1,256,3328]{1,2,0:T(8,128)(2,1)S(1)}, bf16[1,256,3328]{1,2,0:T(8,128)(2,1)S(1)}, u32[]{:S(2)}, u32[]{:S(2)}) %collective-permute-start.4) | collective-permute-done | bytes 1703968 | tf_op jit(solution)/shard_map/ppermute | solution.py:33
  532.3 18.8 %collective-permute-done.5 = bf16[1,256,3328]{1,2,0:T(8,128)(2,1)} collective-permute-done((bf16[1,256,3328]{1,2,0:T(8,128)(2,1)S(1)}, bf16[1,256,3328]{1,2,0:T(8,128)(2,1)}, u32[]{:S(2)}, u32[]{:S(2)}) %collective-permute-start.5) | collective-permute-done | bytes 1703968 | tf_op jit(solution)/shard_map/ppermute | solution.py:33
  554.8 11.9 %copy.15 = bf16[1,2,256,8192]{2,3,1,0:T(8,128)(2,1)} copy(bf16[1,2,256,8192]{3,2,1,0:T(8,128)(2,1)} %param.11) | data formatting | bytes 16777216 | tf_op args[3]
  569.4 9.8 %slice_convert_fusion = f32[2,256,2,13,256]{1,4,3,2,0:T(8,128)} fusion(bf16[2,256,2,16,256]{1,4,3,2,0:T(8,128)(2,1)} %bitcast.100), kind=kLoop, calls=%fused_computation.12 | loop fusion | flops 3407872 | bytes 20447232 | tf_op jit(solution)/shard_map/convert_element_type | solution.py:30
  599.5 55.9 %while.20 = (s32[]{:T(128)}, f32[2,256,2,13,256]{1,4,3,2,0:T(8,128)}, s32[8]{0:T(128)S(1)}, s32[]{:T(128)}, pred[]{:T(512)}, /*index=5*/s32[8,13]{1,0:T(8,128)},...) while((s32[]{:T(128)}, f32[2,256,2,13,256]{1,4,3,2,0:T(8,128)}, ...), condition=%wide.region_15.16_spmd, body=%wide.region_12.15_spmd.sunk | while | flops 5963816 | bytes 32375320 | solution.py:61
  602.0 11.9 %conditional.2 = (f32[2,256,2,13,256]{1,4,3,2,0:T(8,128)}) conditional(s32[]{:T(128)} %convert_element_type.52, f32[2,256,2,13,256]{1,4,3,2,0:T(8,128)} %get-tuple-element.603, (s32[]{:T(128)}, s32[]{:T(128)}, f32[2,256,2,13,256]{1,4,3,2,0:T(8,128)}, s32[8,13]{1,0:T(8,128)}, s32[]{:T(128)}, /*index=5*/bf16[8,256,3328]{1,2,0:T(8,128)(2,1)}, ...), branch_computations={%region_13.13_spmd, %region_14.14_spmd} | conditional | flops 5963810 | bytes 32375100 | solution.py:59
  624.0 12.0 %conditional.2 = (f32[2,256,2,13,256]{1,4,3,2,0:T(8,128)}) conditional(s32[]{:T(128)} %convert_element_type.52, f32[2,256,2,13,256]{1,4,3,2,0:T(8,128)} %get-tuple-element.603, (s32[]{:T(128)}, s32[]{:T(128)}, f32[2,256,2,13,256]{1,4,3,2,0:T(8,128)}, s32[8,13]{1,0:T(8,128)}, s32[]{:T(128)}, /*index=5*/bf16[8,256,3328]{1,2,0:T(8,128)(2,1)}, ...), branch_computations={%region_13.13_spmd, %region_14.14_spmd} | conditional | flops 5963810 | bytes 32375100 | solution.py:59
  638.5 11.9 %conditional.2 = (f32[2,256,2,13,256]{1,4,3,2,0:T(8,128)}) conditional(s32[]{:T(128)} %convert_element_type.52, f32[2,256,2,13,256]{1,4,3,2,0:T(8,128)} %get-tuple-element.603, (s32[]{:T(128)}, s32[]{:T(128)}, f32[2,256,2,13,256]{1,4,3,2,0:T(8,128)}, s32[8,13]{1,0:T(8,128)}, s32[]{:T(128)}, /*index=5*/bf16[8,256,3328]{1,2,0:T(8,128)(2,1)}, ...), branch_computations={%region_13.13_spmd, %region_14.14_spmd} | conditional | flops 5963810 | bytes 32375100 | solution.py:59
  655.4 8.8 %convert_element_type.45 = bf16[2,256,2,13,256]{1,4,3,2,0:T(8,128)(2,1)} convert(f32[2,256,2,13,256]{1,4,3,2,0:T(8,128)} %get-tuple-element.415) | non-fusion elementwise | flops 3407872 | bytes 20447232 | tf_op jit(solution)/shard_map/convert_element_type | solution.py:62
  664.3 6.9 pad_maximum_fusion
  671.2 12.0 %copy.19 = bf16[1,2,256,8192]{3,2,1,0:T(8,128)(2,1)} copy(bf16[1,2,256,8192]{2,3,1,0:T(8,128)(2,1)} %bitcast.101) | data formatting | bytes 16777216 | tf_op jit(solution)/shard_map/broadcast_in_dim;reshape | solution.py:64
  (173 shorter events, 184.5 us)
Async XLA Ops:
  7.2 108.8 %all-gather.2.cloned.1.call-start = ((), (), s32[]{:S(2)}) async-start(), calls=%async_computation | async-start | bytes 13369344 | tf_op jit(solution)/shard_map/all_gather | solution.py:18
  115.9 1.7 slice-start.3
  122.2 1.4 copy-start.16
  340.6 8.6 %copy-start.17 = (f32[6,128,128]{1,2,0:T(8,128)}, f32[6,128,128]{1,2,0:T(8,128)S(1)}, u32[]{:S(2)}) copy-start(f32[6,128,128]{1,2,0:T(8,128)S(1)} %custom-call.51) | copy-start | bytes 1179652
  345.9 14.6 %slice-start = ((s8[12582912]{0:T(1024)(128)(4,1)}), s8[4194304]{0:T(1024)(128)(4,1)S(1)}, s32[]{:S(2)}) async-start(s8[12582912]{0:T(1024)(128)(4,1)} %bitcast.107), calls=%async_computation.1 | async-start | bytes 8388608
  349.2 11.3 %slice-start.1 = ((s8[12582912]{0:T(1024)(128)(4,1)}), s8[4194304]{0:T(1024)(128)(4,1)S(1)}, s32[]{:S(2)}) async-start(s8[12582912]{0:T(1024)(128)(4,1)} %bitcast.107), calls=%async_computation.2 | async-start | bytes 8388608
  351.0 9.6 %slice-start.2 = ((s8[12582912]{0:T(1024)(128)(4,1)}), s8[4194304]{0:T(1024)(128)(4,1)S(1)}, s32[]{:S(2)}) async-start(s8[12582912]{0:T(1024)(128)(4,1)} %bitcast.107), calls=%async_computation.3 | async-start | bytes 8388608
  357.3 3.2 copy-start.1
  360.6 5.2 copy-start.14
  392.5 2.2 copy-start
  394.7 17.5 %copy-start.2 = (f32[256,768]{0,1:T(8,128)}, f32[256,768]{0,1:T(8,128)S(1)}, u32[]{:S(2)}) copy-start(f32[256,768]{0,1:T(8,128)S(1)} %fusion.30) | copy-start | bytes 2359300
  412.2 20.5 %collective-permute-start = (bf16[1,256,3328]{1,2,0:T(8,128)(2,1)S(1)}, bf16[1,256,3328]{1,2,0:T(8,128)(2,1)S(1)}, u32[]{:S(2)}, u32[]{:S(2)}) collective-permute-start(bf16[1,256,3328]{1,2,0:T(8,128)(2,1)S(1)} %fusion.16), channel_id=1, source_target_pairs={{0,16},{16,32},{32,48},{48,64},{64,80},{80,96},{96,112},{112,0},{1... | collective-permute-start | bytes 5111816 | tf_op jit(solution)/shard_map/ppermute | solution.py:33
  432.7 1.2 copy-start.4
  433.9 22.5 %collective-permute-start.1 = (bf16[1,256,3328]{1,2,0:T(8,128)(2,1)S(1)}, bf16[1,256,3328]{1,2,0:T(8,128)(2,1)S(1)}, u32[]{:S(2)}, u32[]{:S(2)}) collective-permute-start(bf16[1,256,3328]{1,2,0:T(8,128)(2,1)S(1)} %collective-permute-done), channel_id=1, source_target_pairs={{0,16},{16,32},{32,48},{48,64},{64,80},{80,96},{96,112},{112,0},{1... | collective-permute-start | bytes 5111816 | tf_op jit(solution)/shard_map/ppermute | solution.py:33
  456.4 1.2 copy-start.6
  457.6 22.5 %collective-permute-start.2 = (bf16[1,256,3328]{1,2,0:T(8,128)(2,1)S(1)}, bf16[1,256,3328]{1,2,0:T(8,128)(2,1)S(1)}, u32[]{:S(2)}, u32[]{:S(2)}) collective-permute-start(bf16[1,256,3328]{1,2,0:T(8,128)(2,1)S(1)} %collective-permute-done.1), channel_id=1, source_target_pairs={{0,16},{16,32},{32,48},{48,64},{64,80},{80,96},{96,112},{112,0},{1... | collective-permute-start | bytes 5111816 | tf_op jit(solution)/shard_map/ppermute | solution.py:33
  480.0 1.2 copy-start.8
  481.3 22.5 %collective-permute-start.3 = (bf16[1,256,3328]{1,2,0:T(8,128)(2,1)S(1)}, bf16[1,256,3328]{1,2,0:T(8,128)(2,1)S(1)}, u32[]{:S(2)}, u32[]{:S(2)}) collective-permute-start(bf16[1,256,3328]{1,2,0:T(8,128)(2,1)S(1)} %collective-permute-done.2), channel_id=1, source_target_pairs={{0,16},{16,32},{32,48},{48,64},{64,80},{80,96},{96,112},{112,0},{1... | collective-permute-start | bytes 5111816 | tf_op jit(solution)/shard_map/ppermute | solution.py:33
  503.7 1.2 copy-start.10
  504.9 22.5 %collective-permute-start.4 = (bf16[1,256,3328]{1,2,0:T(8,128)(2,1)S(1)}, bf16[1,256,3328]{1,2,0:T(8,128)(2,1)S(1)}, u32[]{:S(2)}, u32[]{:S(2)}) collective-permute-start(bf16[1,256,3328]{1,2,0:T(8,128)(2,1)S(1)} %collective-permute-done.3), channel_id=1, source_target_pairs={{0,16},{16,32},{32,48},{48,64},{64,80},{80,96},{96,112},{112,0},{1... | collective-permute-start | bytes 5111816 | tf_op jit(solution)/shard_map/ppermute | solution.py:33
  527.4 1.2 copy-start.12
  528.6 22.5 %collective-permute-start.5 = (bf16[1,256,3328]{1,2,0:T(8,128)(2,1)S(1)}, bf16[1,256,3328]{1,2,0:T(8,128)(2,1)}, u32[]{:S(2)}, u32[]{:S(2)}) collective-permute-start(bf16[1,256,3328]{1,2,0:T(8,128)(2,1)S(1)} %collective-permute-done.4), channel_id=1, source_target_pairs={{0,16},{16,32},{32,48},{48,64},{64,80},{80,96},{96,112},{112,0},{1... | collective-permute-start | bytes 5111816 | tf_op jit(solution)/shard_map/ppermute | solution.py:33
  551.0 29.3 %collective-permute-start.6 = (bf16[1,256,3328]{1,2,0:T(8,128)(2,1)}, bf16[1,256,3328]{1,2,0:T(8,128)(2,1)}, u32[]{:S(2)}, u32[]{:S(2)}) collective-permute-start(bf16[1,256,3328]{1,2,0:T(8,128)(2,1)} %collective-permute-done.5), channel_id=1, source_target_pairs={{0,16},{16,32},{32,48},{48,64},{64,80},{80,96},{96,112},{112,0},{1... | collective-permute-start | bytes 5111816 | tf_op jit(solution)/shard_map/ppermute | solution.py:33
  569.4 9.8 %copy-start.3 = (f32[256,768]{0,1:T(8,128)S(1)}, f32[256,768]{0,1:T(8,128)}, u32[]{:S(2)}) copy-start(f32[256,768]{0,1:T(8,128)} %copy-done.2) | copy-start | bytes 2359300
  581.9 2.0 copy-start.13
  583.9 1.5 copy-start.11
  585.3 1.5 copy-start.9
  586.8 1.5 copy-start.7
  588.2 1.5 copy-start.5
  593.8 5.8 copy-start.18
  655.4 8.8 %copy-start.15 = (bf16[2,256,2,3,256]{1,4,3,2,0:T(8,128)(2,1)S(1)}, bf16[2,256,2,3,256]{1,4,3,2,0:T(8,128)(2,1)}, u32[]{:S(2)}) copy-start(bf16[2,256,2,3,256]{1,4,3,2,0:T(8,128)(2,1)} %slice.203) | copy-start | bytes 4718596
Sparse Core Ops, SparseCore 0:
  15.0 100.8 all-gather.1
